TPU v7x, 32 devices: a whole 2x2x4 slice. The times are simulated.
32 devices in a mesh: dp: 8 (over y, x, core), tensor: 4 (over z).
Axes of the slice: x: 2, y: 2, z: 4, core: 2. Of those that a mesh axis runs over, the one named last changes fastest.
Arguments:
- kv_cache: bfloat16 [64, 512, 2048], P('dp', None, 'tensor'), may hold values from -4 to 4
- new_kv: bfloat16 [4, 64, 2048], P(None, 'dp', 'tensor'), may hold values from -4 to 4
- queries: bfloat16 [4, 64, 8192], P(None, 'dp', 'tensor'), may hold values from -80 to 80
- verify_q: bfloat16 [16, 512, 8192], P('dp', None, 'tensor'), may hold values from -80 to 80
- prompt_kv: bfloat16 [8, 256, 2048], P('dp', None, 'tensor'), may hold values from -4 to 4
- readout: bfloat16 [8192], P('tensor'), may hold values from -0.1875 to 0.1875
- finish: int32 [64], replicated, may hold values from 0 to 4, as said below
- dest: int32 [64], replicated, may hold values from -1 to 15, as said below
- prompt: int32 [64], replicated, may hold values from -1 to 7, as said below
- lengths: int32 [64], replicated, may hold values from 2 to 508
Outputs:
- decoded: bfloat16 [4, 64, 8192], P(None, 'dp', 'tensor')
- new_cache: bfloat16 [64, 512, 2048], P('dp', None, 'tensor')
- rewards: float32 [16, 512], P('dp', 'tensor')
Inputs may be any that keep to these rules, and one draw needn't show every extreme that they name: 4 marks a row that does not finish; rows with a smaller value are finished candidates; at most 2 rows of one dp index finish, and in every draw some dp index has exactly 2 finished rows. `dest`: -1 exactly for rows that do not finish; no verifier slot receives two rows; the finished rows of one dp index go to slots of distinct dp indices; in every draw some dp index has all 2 of its slots filled. `prompt`: -1 exactly for rows that do not finish.
All inputs are finite; a program needn't handle non-finite values.
Results may differ from a plain program's by a relative error of at most 0.007.
Values may be sent and summed in bfloat16 or wider, within the bound.
A program may use at most 192 MiB of HBM per device.

v0:
```python
import math

import jax
import jax.numpy as jnp
from jax import lax
from jax.sharding import PartitionSpec as P

GROUP = 8
D_HEAD = 128
HALF = 64


def from_partner(value, axis, apart):
    mask = 2**apart
    pairs = [(source, source ^ mask) for source in range(lax.axis_size(axis))]
    return lax.ppermute(value, axis, pairs)


def attend(query_full, keys_full, values_full, weight_full, slot_span):
    context_len = query_full.shape[0]
    query_pos = jnp.arange(context_len)[:, None]
    key_pos = jnp.arange(context_len)[None, :]
    scores = jnp.einsum("thgd,phd->hgtp", query_full, keys_full, preferred_element_type=jnp.float32)
    scores = scores * (1.0 / math.sqrt(D_HEAD))
    allowed = (key_pos <= query_pos) & (key_pos < jnp.maximum(slot_span, 1))
    scores = jnp.where(allowed, scores, -jnp.inf)
    slot_top = jnp.max(scores, axis=-1, keepdims=True)
    exp_scores = jnp.exp(scores - slot_top)
    prob_weights = (exp_scores / jnp.sum(exp_scores, axis=-1, keepdims=True)).astype(jnp.bfloat16)
    attended = jnp.einsum(
        "hgtp,phd->thgd", prob_weights, values_full, preferred_element_type=jnp.float32
    )
    reward_row = jnp.einsum(
        "thgd,hgd->t", attended, weight_full.astype(jnp.float32), precision=lax.Precision.HIGHEST
    )
    return jnp.where(jnp.arange(context_len) < slot_span, reward_row, 0.0)


def ordered(pair_side, mine_part, other_part):
    low_part = jnp.where(pair_side == 0, mine_part, other_part)
    high_part = jnp.where(pair_side == 0, other_part, mine_part)
    return jnp.concatenate([low_part, high_part], axis=-1)


def body(kv_cache, new_kv, queries, verify_q, prompt_kv, readout, finish, dest, prompt, lengths):
    row_count = kv_cache.shape[0]
    context_len = kv_cache.shape[1]
    step_count = new_kv.shape[0]
    slot_count = verify_q.shape[0]
    plen_local = prompt_kv.shape[1]
    kv_local = kv_cache.shape[2] // (2 * HALF)
    tp_size = lax.axis_size("tensor")
    peer_count = lax.axis_size("dp")
    my_index = lax.axis_index("dp")
    pair_side = lax.axis_index("tensor") // (tp_size // 2)
    pair_bit = tp_size.bit_length() - 2
    first_row = my_index * row_count
    my_finish = lax.dynamic_slice_in_dim(finish, first_row, row_count)
    my_dest = lax.dynamic_slice_in_dim(dest, first_row, row_count)
    my_prompt = lax.dynamic_slice_in_dim(prompt, first_row, row_count)
    my_length = lax.dynamic_slice_in_dim(lengths, first_row, row_count)
    query_half = queries.reshape(step_count, row_count, kv_local, GROUP, HALF)
    cache_local = kv_cache.reshape(row_count, context_len, kv_local, 2, HALF)
    keys_old = cache_local[:, :, :, 0, :]
    values_old = cache_local[:, :, :, 1, :]
    fresh_kv = new_kv.reshape(step_count, row_count, kv_local, 2, HALF)
    keys_new = fresh_kv[:, :, :, 0, :]
    values_new = fresh_kv[:, :, :, 1, :]
    score_scale = 1.0 / math.sqrt(D_HEAD)
    part_old = jnp.einsum(
        "srhgd,rphd->srhgp", query_half, keys_old, preferred_element_type=jnp.float32
    )
    part_new = jnp.einsum(
        "srhgd,trhd->srhgt", query_half, keys_new, preferred_element_type=jnp.float32
    )
    other_old, other_new = from_partner((part_old, part_new), "tensor", pair_bit)
    score_old = (part_old + other_old) * score_scale
    score_new = (part_new + other_new) * score_scale
    position = jnp.arange(context_len)
    steps_seen = jnp.arange(step_count)
    old_valid = (position[None, :] < my_length[:, None])[None, :, None, None, :]
    new_valid = (steps_seen[None, :] <= steps_seen[:, None])[:, None, None, None, :]
    score_old = jnp.where(old_valid, score_old, -jnp.inf)
    score_new = jnp.where(new_valid, score_new, -jnp.inf)
    row_top = jnp.maximum(
        jnp.max(score_old, axis=-1, keepdims=True), jnp.max(score_new, axis=-1, keepdims=True)
    )
    exp_old = jnp.exp(score_old - row_top)
    exp_new = jnp.exp(score_new - row_top)
    exp_total = jnp.sum(exp_old, axis=-1, keepdims=True) + jnp.sum(exp_new, axis=-1, keepdims=True)
    prob_old = (exp_old / exp_total).astype(jnp.bfloat16)
    prob_new = (exp_new / exp_total).astype(jnp.bfloat16)
    mixed_out = jnp.einsum(
        "srhgp,rphd->srhgd", prob_old, values_old, preferred_element_type=jnp.float32
    )
    mixed_out = mixed_out + jnp.einsum(
        "srhgt,trhd->srhgd", prob_new, values_new, preferred_element_type=jnp.float32
    )
    live_step = (steps_seen[:, None] <= my_finish[None, :])[:, :, None, None, None]
    mixed_out = jnp.where(live_step, mixed_out, 0.0)
    decoded = mixed_out.reshape(step_count, row_count, kv_local * GROUP * HALF).astype(jnp.bfloat16)
    final_cache = kv_cache
    for step_index in range(step_count):
        hit_mask = (position[None, :] == my_length[:, None] + step_index) & (
            step_index <= my_finish[:, None]
        )
        final_cache = jnp.where(hit_mask[:, :, None], new_kv[step_index][:, None, :], final_cache)
    finished_row = my_finish < step_count
    wanted = my_index * slot_count + jnp.arange(slot_count)
    dest_table = dest.reshape(peer_count, row_count)
    slot_hits = dest_table[None, :, :] == wanted[:, None, None]
    full_span = (lengths + finish + 1).reshape(peer_count, row_count)
    span_len = jnp.sum(jnp.where(slot_hits, full_span[None, :, :], 0), axis=(1, 2))
    target_dev = jnp.where(finished_row, my_dest // slot_count, -1)
    pick_rows = (target_dev[None, :] == jnp.arange(peer_count)[:, None]).astype(jnp.bfloat16)
    outgoing = jnp.einsum(
        "er,rcx->ecx", pick_rows, final_cache, preferred_element_type=jnp.float32
    ).astype(jnp.bfloat16)
    incoming = lax.all_to_all(outgoing, "dp", split_axis=0, concat_axis=0, tiled=True)
    chosen = jnp.any(slot_hits, axis=2).astype(jnp.bfloat16)
    received = jnp.einsum(
        "ve,ecx->vcx", chosen, incoming, preferred_element_type=jnp.float32
    ).astype(jnp.bfloat16)
    verify_local = verify_q.reshape(slot_count, context_len, kv_local, GROUP, HALF)
    slot_cache = received.reshape(slot_count, context_len, kv_local, 2, HALF)
    half_group = GROUP // 2
    split_query = verify_local.reshape(slot_count, context_len, kv_local, 2, half_group, HALF)
    keep_query = lax.dynamic_index_in_dim(split_query, pair_side, 3, keepdims=False)
    give_query = lax.dynamic_index_in_dim(split_query, 1 - pair_side, 3, keepdims=False)
    split_weight = readout.reshape(kv_local, 2, half_group, HALF)
    keep_weight = lax.dynamic_index_in_dim(split_weight, pair_side, 1, keepdims=False)
    give_weight = lax.dynamic_index_in_dim(split_weight, 1 - pair_side, 1, keepdims=False)
    other_query, other_slots, other_weight = from_partner(
        (give_query, received, give_weight), "tensor", pair_bit
    )
    other_cache = other_slots.reshape(slot_count, context_len, kv_local, 2, HALF)
    query_full = ordered(pair_side, keep_query, other_query)
    keys_full = ordered(pair_side, slot_cache[:, :, :, 0, :], other_cache[:, :, :, 0, :])
    values_full = ordered(pair_side, slot_cache[:, :, :, 1, :], other_cache[:, :, :, 1, :])
    weight_full = ordered(pair_side, keep_weight, other_weight)

    def slot_reward(arguments):
        return attend(arguments[0], arguments[1], arguments[2], weight_full, arguments[3])

    partial_value = lax.map(slot_reward, (query_full, keys_full, values_full, span_len))
    rewards = lax.psum_scatter(partial_value, "tensor", scatter_dimension=1, tiled=True)
    shard_piece = lax.all_gather(prompt_kv, "dp", axis=0, tiled=True)
    piece_rows = shard_piece.shape[0]
    prompt_match = (my_prompt[:, None] == jnp.arange(piece_rows)[None, :]).astype(jnp.bfloat16)
    added = jnp.einsum("rn,nlx->rlx", prompt_match, shard_piece, preferred_element_type=jnp.float32)
    refill = added.astype(jnp.bfloat16)
    padded = jnp.concatenate(
        [refill, jnp.zeros((row_count, context_len - plen_local, kv_cache.shape[2]), jnp.bfloat16)],
        axis=1,
    )
    new_cache = jnp.where(finished_row[:, None, None], padded, final_cache)
    return (decoded, new_cache, rewards)


def solution(mesh):
    placed = (
        P("dp", None, "tensor"),
        P(None, "dp", "tensor"),
        P(None, "dp", "tensor"),
        P("dp", None, "tensor"),
        P("dp", None, "tensor"),
        P("tensor"),
        P(),
        P(),
        P(),
        P(),
    )
    return jax.shard_map(
        body,
        mesh=mesh,
        in_specs=placed,
        out_specs=(P(None, "dp", "tensor"), P("dp", None, "tensor"), P("dp", "tensor")),
        check_vma=False,
    )
```

profile of v0, /device:TPU:6, one launch (start us, length us, event | category | flops | bytes accessed | tf_op | source)
XLA Modules:
  0.0 401.3 jit_solution(7710049466535013782)
XLA Ops:
  11.2 11.7 %convolution_convert_fusion = bf16[8,512,512]{2,0,1:T(8,128)(2,1)S(1)} fusion(bf16[8,512,512]{2,1,0:T(8,128)(2,1)} %param.12, pred[8,512]{0,1:T(8,128)(4,1)S(1)} %copy.109, pred[8,512]{0,1:T(8,128)(4,1)S(1)} %fusion.51, pred[8,512]{0,1:T(8,128)(4,1)S(1)} %fusion.50, pred[8,512]{0,1:T(8,128)(4,1)S(1)} %fusion.49, bf16[8,512]{1,0:T(8,128)(2,1)S(1)} %get-tuple-element.124, ...), kind=kOutput, calls=%fused_computation.37 | convolution fusion | flops 44040256 | bytes 8437792 | tf_op jit(solution)/shard_map/er,rcx->ecx/dot_general | solution.py:116
  22.9 3.4 copy.111
  26.3 4.5 %all-to-all-start = ((bf16[8,512,512]{2,1,0:T(8,128)(2,1)}), bf16[8,512,512]{2,1,0:T(8,128)(2,1)}, u32[]{:S(2)}, u32[]{:S(2)}) async-start(bf16[8,512,512]{2,1,0:T(8,128)(2,1)} %copy.111), calls=%async_computation | async-start | bytes 8388608 | tf_op jit(solution)/shard_map/all_to_all | solution.py:119
  30.9 6.5 %copy.100 = bf16[8,512,512]{1,2,0:T(8,128)(2,1)} copy(bf16[8,512,512]{2,1,0:T(8,128)(2,1)} %param.12) | data formatting | bytes 8388608 | tf_op args[0]
  37.6 2.0 fusion.36
  39.7 3.1 collective-permute-start
  42.7 6.2 %copy.121 = bf16[2,512,2048]{1,2,0:T(8,128)(2,1)} copy(bf16[2,512,2048]{2,1,0:T(8,128)(2,1)} %param.15) | data formatting | bytes 8388608 | tf_op args[3]
  49.0 3.2 dynamic-slice_bitcast_fusion
  52.3 2.9 collective-permute-start.4
  57.8 171.9 %collective-permute-done.4 = bf16[4,4,64]{2,1,0:T(4,128)(2,1)S(1)} collective-permute-done((bf16[4,4,64]{2,1,0:T(4,128)(2,1)S(1)}, bf16[4,4,64]{2,1,0:T(4,128)(2,1)S(1)}, u32[]{:S(2)}, u32[]{:S(2)}) %collective-permute-start.4) | collective-permute-done | bytes 2080 | tf_op jit(solution)/shard_map/ppermute | solution.py:16
  229.9 5.0 %collective-permute-done.1 = f32[4,8,4,8,4]{3,4,0,2,1:T(4,128)S(1)} collective-permute-done((f32[4,8,4,8,4]{3,4,0,2,1:T(4,128)S(1)}, f32[4,8,4,8,4]{3,4,0,2,1:T(4,128)S(1)}, u32[]{:S(2)}, u32[]{:S(2)}) %collective-permute-start.1) | collective-permute-done | bytes 16416 | tf_op jit(solution)/shard_map/ppermute | solution.py:16
  235.2 2.0 fusion.69
  240.5 5.1 %fusion.38 = bf16[2,512,512]{2,0,1:T(2,128)(2,1)S(1)} fusion(bf16[8,512,512]{2,1,0:T(8,128)(2,1)} %all-to-all-done, pred[2,8]{1,0:T(4,128)(4,1)S(1)} %compare_reduce_fusion), kind=kOutput, calls=%fused_computation.53 | convolution fusion | flops 8912896 | bytes 5242896 | tf_op jit(solution)/shard_map/ve,ecx->vcx/dot_general | solution.py:121
  248.0 2.5 bitcast_select_fusion.5
  250.5 2.5 pad_maximum_fusion
  252.9 1.4 copy.113
  254.4 4.2 %fusion.32 = bf16[8,256,512]{2,0,1:T(8,128)(2,1)} fusion(bf16[8,256,512]{2,1,0:T(8,128)(2,1)} %all-gather.2.cloned.1.call-done, s32[8]{0:T(128)S(1)} %dynamic_slice.43), kind=kOutput, calls=%fused_computation.50 | convolution fusion | flops 17825856 | bytes 4194336 | tf_op jit(solution)/shard_map/rn,nlx->rlx/dot_general | solution.py:150
  258.6 35.2 %collective-permute-done.2 = bf16[2,512,512]{2,0,1:T(2,128)(2,1)} collective-permute-done((bf16[2,512,512]{2,0,1:T(2,128)(2,1)S(1)}, bf16[2,512,512]{2,0,1:T(2,128)(2,1)}, u32[]{:S(2)}, u32[]{:S(2)}) %collective-permute-start.2) | collective-permute-done | bytes 1048608 | tf_op jit(solution)/shard_map/ppermute | solution.py:16
  293.8 2.4 copy.115
  297.7 75.4 %while.10 = (s32[]{:T(128)}, f32[2,512]{1,0:T(2,128)S(1)}, s32[2]{0:T(128)S(1)}, bf16[2,512,4,128]{1,3,2,0:T(8,128)(2,1)}, bf16[2,512,4,128]{1,3,2,0:T(8,128)(2,...) while((s32[]{:T(128)}, f32[2,512]{1,0:T(2,128)S(1)}, ...), condition=%wide.region_9.10_spmd, body=%wide.region_6.9_spmd.sunk | while | flops 2194147328 | bytes 83443872 | solution.py:145
  297.7 9.8 %fusion.88 = f32[4,512,512,4]{2,1,3,0:T(8,128)} fusion(bf16[2,512,4,4,128]{1,4,3,2,0:T(8,128)(2,1)} %get-tuple-element.209, s32[]{:T(128)} %get-tuple-element.195, bf16[2,512,4,128]{1,3,2,0:T(8,128)(2,1)S(1)} %get-tuple-element.208), kind=kOutput, calls=%fused_computation.12.clone.1 | convolution fusion | flops 1073741824 | bytes 19399680 | tf_op jit(solution)/shard_map/while/body/eval_jaxpr/thgd,phd->hgtp/dot_general | solution.py:23
  309.0 17.6 %fusion.90 = (f32[4,4,512]{2,1,0:T(4,128)S(1)}, f32[4,4,512,512]{2,3,1,0:T(8,128)}) fusion(f32[4,512,512,4]{2,1,3,0:T(8,128)} %fusion.88, pred[512,512]{0,1:T(8,128)(4,1)S(1)} %fusion.89), kind=kOutput, calls=%fused_computation.128.clone.1 | output fusion | flops 25166336 | bytes 33849344 | tf_op jit(solution)/shard_map/while/body/eval_jaxpr/sub | solution.py:28
  326.6 6.6 %fusion.91 = f32[512,4,4,128]{0,3,2,1:T(8,128)S(1)} fusion(f32[4,4,512,512]{2,3,1,0:T(8,128)} %get-tuple-element.184, f32[4,4,512]{2,1,0:T(4,128)S(1)} %get-tuple-element.185, bf16[2,512,4,128]{1,3,2,0:T(8,128)(2,1)S(1)} %copy-done.4, s32[]{:T(128)} %get-tuple-element.195), kind=kOutput, calls=%fused_computation.11.clone.1 | convolution fusion | flops 1082130432 | bytes 21528580 | tf_op jit(solution)/shard_map/while/body/eval_jaxpr/hgtp,phd->thgd/dot_general | solution.py:30
  333.2 1.5 fusion.92
  335.4 9.7 %fusion.88 = f32[4,512,512,4]{2,1,3,0:T(8,128)} fusion(bf16[2,512,4,4,128]{1,4,3,2,0:T(8,128)(2,1)} %get-tuple-element.209, s32[]{:T(128)} %get-tuple-element.195, bf16[2,512,4,128]{1,3,2,0:T(8,128)(2,1)S(1)} %get-tuple-element.208), kind=kOutput, calls=%fused_computation.12.clone.1 | convolution fusion | flops 1073741824 | bytes 19399680 | tf_op jit(solution)/shard_map/while/body/eval_jaxpr/thgd,phd->hgtp/dot_general | solution.py:23
  346.6 17.6 %fusion.90 = (f32[4,4,512]{2,1,0:T(4,128)S(1)}, f32[4,4,512,512]{2,3,1,0:T(8,128)}) fusion(f32[4,512,512,4]{2,1,3,0:T(8,128)} %fusion.88, pred[512,512]{0,1:T(8,128)(4,1)S(1)} %fusion.89), kind=kOutput, calls=%fused_computation.128.clone.1 | output fusion | flops 25166336 | bytes 33849344 | tf_op jit(solution)/shard_map/while/body/eval_jaxpr/sub | solution.py:28
  364.2 6.6 %fusion.91 = f32[512,4,4,128]{0,3,2,1:T(8,128)S(1)} fusion(f32[4,4,512,512]{2,3,1,0:T(8,128)} %get-tuple-element.184, f32[4,4,512]{2,1,0:T(4,128)S(1)} %get-tuple-element.185, bf16[2,512,4,128]{1,3,2,0:T(8,128)(2,1)S(1)} %copy-done.4, s32[]{:T(128)} %get-tuple-element.195), kind=kOutput, calls=%fused_computation.11.clone.1 | convolution fusion | flops 1082130432 | bytes 21528580 | tf_op jit(solution)/shard_map/while/body/eval_jaxpr/hgtp,phd->thgd/dot_general | solution.py:30
  370.8 1.5 fusion.92
  374.0 9.1 %pad_select_fusion = bf16[8,512,512]{2,0,1:T(8,128)(2,1)S(1)} fusion(bf16[8,256,512]{2,0,1:T(8,128)(2,1)S(1)} %copy-done.1, pred[8]{0:T(512)(128)(4,1)S(1)} %copy-done.24, bf16[8,512,512]{2,1,0:T(8,128)(2,1)} %param.12, bf16[8,512]{1,0:T(8,128)(2,1)S(1)} %copy-done.20, pred[8,512]{0,1:T(8,128)(4,1)S(1)} %copy-done.6, bf16[8,512]{1,0:T(8,128)(2,1)S(1)} %copy-done.22, ...), kind=kLoop, calls=%fused_computation.36 | loop fusion | flops 10485760 | bytes 10534920 | tf_op jit(solution)/shard_map/jit(_where)/select_n | solution.py:156
  383.1 3.5 copy.124
  386.5 5.9 %reduce-scatter.4.cloned.1.call-done = f32[128,2]{1,0:T(8,128)} async-done(((f32[512,2]{1,0:T(8,128)}), f32[128,2]{1,0:T(8,128)}) %reduce-scatter.4.cloned.1.call-update) | async-done | bytes 1040
  392.4 1.5 copy.136
  (124 shorter events, 17.2 us)
Async XLA Ops:
  9.5 13.4 %copy-start.5 = (pred[8,512]{0,1:T(8,128)(4,1)}, pred[8,512]{0,1:T(8,128)(4,1)S(1)}, u32[]{:S(2)}) copy-start(pred[8,512]{0,1:T(8,128)(4,1)S(1)} %copy.109) | copy-start | bytes 12292
  26.3 214.1 %all-to-all-start = ((bf16[8,512,512]{2,1,0:T(8,128)(2,1)}), bf16[8,512,512]{2,1,0:T(8,128)(2,1)}, u32[]{:S(2)}, u32[]{:S(2)}) async-start(bf16[8,512,512]{2,1,0:T(8,128)(2,1)} %copy.111), calls=%async_computation | async-start | bytes 8388608 | tf_op jit(solution)/shard_map/all_to_all | solution.py:119
  30.9 6.5 %copy-start.13 = (bf16[4,8,2048]{2,1,0:T(8,128)(2,1)S(1)}, bf16[4,8,2048]{2,1,0:T(8,128)(2,1)}, u32[]{:S(2)}) copy-start(bf16[4,8,2048]{2,1,0:T(8,128)(2,1)} %param.14) | copy-start | bytes 393220
  30.9 223.5 %all-gather.2.cloned.1.call-start = ((), (), s32[]{:S(2)}) async-start(), calls=%async_computation.2 | async-start | bytes 2359296 | tf_op jit(solution)/shard_map/all_gather | solution.py:147
  39.7 195.5 %collective-permute-start = (f32[4,8,4,8,512]{4,3,0,2,1:T(8,128)S(1)}, f32[4,8,4,8,512]{4,3,0,2,1:T(8,128)}, u32[]{:S(2)}, u32[]{:S(2)}) collective-permute-start(f32[4,8,4,8,512]{4,3,0,2,1:T(8,128)S(1)} %fusion.36), channel_id=1, source_target_pairs={{0,2},{1,3},{2,0},{3,1},{4,6},{5,7},{6,4},{7,5},{8,10},{9,11},{10,... | collective-permute-start | bytes 6291464 | tf_op jit(solution)/shard_map/ppermute | solution.py:16
  48.9 3.3 copy-start.23
  48.9 6.3 %copy-start.14 = (bf16[4,8,512]{2,1,0:T(8,128)(2,1)S(1)}, bf16[4,8,512]{2,1,0:T(8,128)(2,1)}, u32[]{:S(2)}) copy-start(bf16[4,8,512]{2,1,0:T(8,128)(2,1)} %param.13) | copy-start | bytes 98308
  48.9 8.1 %copy-start.26 = (s32[64]{0:T(128)S(1)}, s32[64]{0:T(128)}, u32[]{:S(2)}) copy-start(s32[64]{0:T(128)} %param.18) | copy-start | bytes 772
  48.9 8.1 %copy-start.27 = (s32[64]{0:T(128)S(1)}, s32[64]{0:T(128)}, u32[]{:S(2)}) copy-start(s32[64]{0:T(128)} %param.21) | copy-start | bytes 772
  48.9 8.1 %copy-start.25 = (s32[64]{0:T(128)S(1)}, s32[64]{0:T(128)}, u32[]{:S(2)}) copy-start(s32[64]{0:T(128)} %param.19) | copy-start | bytes 772
  49.0 8.8 %copy-start.28 = (s32[64]{0:T(128)S(1)}, s32[64]{0:T(128)}, u32[]{:S(2)}) copy-start(s32[64]{0:T(128)} %param.20) | copy-start | bytes 772
  52.2 195.8 %collective-permute-start.3 = (bf16[2,512,4,4,64]{1,4,3,2,0:T(8,128)(2,1)}, bf16[2,512,4,4,64]{1,4,3,2,0:T(8,128)(2,1)}, u32[]{:S(2)}, u32[]{:S(2)}) collective-permute-start(bf16[2,512,4,4,64]{1,4,3,2,0:T(8,128)(2,1)} %dynamic-slice_bitcast_fusion), channel_id=1, source_target_pairs={{0,2},{1,3},{2,0},{3,1},{4,6},{5,7},{6,4},{7,5},{8,10},{9,11},{10,... | collective-permute-start | bytes 6291464 | tf_op jit(solution)/shard_map/ppermute | solution.py:16
  52.3 177.5 %collective-permute-start.4 = (bf16[4,4,64]{2,1,0:T(4,128)(2,1)S(1)}, bf16[4,4,64]{2,1,0:T(4,128)(2,1)S(1)}, u32[]{:S(2)}, u32[]{:S(2)}) collective-permute-start(bf16[4,4,64]{2,1,0:T(4,128)(2,1)S(1)} %dynamic-slice_bitcast_fusion.1), channel_id=1, source_target_pairs={{0,2},{1,3},{2,0},{3,1},{4,6},{5,7},{6,4},{7,5},{8,10},{9,11},{10,... | collective-permute-start | bytes 6152 | tf_op jit(solution)/shard_map/ppermute | solution.py:16
  56.7 178.2 %collective-permute-start.1 = (f32[4,8,4,8,4]{3,4,0,2,1:T(4,128)S(1)}, f32[4,8,4,8,4]{3,4,0,2,1:T(4,128)S(1)}, u32[]{:S(2)}, u32[]{:S(2)}) collective-permute-start(f32[4,8,4,8,4]{3,4,0,2,1:T(4,128)S(1)} %convolution_bitcast_fusion), channel_id=1, source_target_pairs={{0,2},{1,3},{2,0},{3,1},{4,6},{5,7},{6,4},{7,5},{8,10},{9,11},{10,... | collective-permute-start | bytes 49160 | tf_op jit(solution)/shard_map/ppermute | solution.py:16
  56.8 335.6 %reduce-scatter.4.cloned.1.call-start = ((), (), s32[]{:S(2)}) async-start(), calls=%async_computation.3 | async-start | bytes 327680
  237.2 1.3 copy-start.2
  239.3 6.4 %copy-start.3 = (f32[4,8,4,8,512]{4,3,0,2,1:T(8,128)S(1)}, f32[4,8,4,8,512]{4,3,0,2,1:T(8,128)}, u32[]{:S(2)}) copy-start(f32[4,8,4,8,512]{4,3,0,2,1:T(8,128)} %copy-done.2) | copy-start | bytes 6291460
  240.5 5.2 %copy-start = (bf16[8,512,512]{1,2,0:T(8,128)(2,1)S(1)}, bf16[8,512,512]{1,2,0:T(8,128)(2,1)}, u32[]{:S(2)}) copy-start(bf16[8,512,512]{1,2,0:T(8,128)(2,1)} %copy.100) | copy-start | bytes 12582916
  240.5 5.2 %copy-start.29 = (f32[8,4,4,8,64]{4,3,2,1,0:T(8,128)S(1)}, f32[8,4,4,8,64]{4,3,2,1,0:T(8,128)}, u32[]{:S(2)}) copy-start(f32[8,4,4,8,64]{4,3,2,1,0:T(8,128)} %fusion.55) | copy-start | bytes 786436
  245.6 48.2 %collective-permute-start.2 = (bf16[2,512,512]{2,0,1:T(2,128)(2,1)S(1)}, bf16[2,512,512]{2,0,1:T(2,128)(2,1)}, u32[]{:S(2)}, u32[]{:S(2)}) collective-permute-start(bf16[2,512,512]{2,0,1:T(2,128)(2,1)S(1)} %fusion.38), channel_id=1, source_target_pairs={{0,2},{1,3},{2,0},{3,1},{4,6},{5,7},{6,4},{7,5},{8,10},{9,11},{10,... | collective-permute-start | bytes 3145736 | tf_op jit(solution)/shard_map/ppermute | solution.py:16
  297.6 76.3 %copy-start.1 = (bf16[8,256,512]{2,0,1:T(8,128)(2,1)S(1)}, bf16[8,256,512]{2,0,1:T(8,128)(2,1)}, u32[]{:S(2)}) copy-start(bf16[8,256,512]{2,0,1:T(8,128)(2,1)} %fusion.32) | copy-start | bytes 6291460
  297.6 76.3 %copy-start.6 = (pred[8,512]{0,1:T(8,128)(4,1)S(1)}, pred[8,512]{0,1:T(8,128)(4,1)}, u32[]{:S(2)}) copy-start(pred[8,512]{0,1:T(8,128)(4,1)} %copy-done.5) | copy-start | bytes 12292
  297.6 76.3 %copy-start.8 = (pred[8,512]{0,1:T(8,128)(4,1)S(1)}, pred[8,512]{0,1:T(8,128)(4,1)}, u32[]{:S(2)}) copy-start(pred[8,512]{0,1:T(8,128)(4,1)} %copy-done.7) | copy-start | bytes 12292
  297.6 76.4 %copy-start.10 = (pred[8,512]{0,1:T(8,128)(4,1)S(1)}, pred[8,512]{0,1:T(8,128)(4,1)}, u32[]{:S(2)}) copy-start(pred[8,512]{0,1:T(8,128)(4,1)} %copy-done.9) | copy-start | bytes 12292
  297.6 76.4 %copy-start.12 = (pred[8,512]{0,1:T(8,128)(4,1)S(1)}, pred[8,512]{0,1:T(8,128)(4,1)}, u32[]{:S(2)}) copy-start(pred[8,512]{0,1:T(8,128)(4,1)} %copy-done.11) | copy-start | bytes 12292
  297.6 76.4 %copy-start.16 = (bf16[8,512]{1,0:T(8,128)(2,1)S(1)}, bf16[8,512]{1,0:T(8,128)(2,1)}, u32[]{:S(2)}) copy-start(bf16[8,512]{1,0:T(8,128)(2,1)} %copy-done.15) | copy-start | bytes 24580
  297.6 76.4 %copy-start.18 = (bf16[8,512]{1,0:T(8,128)(2,1)S(1)}, bf16[8,512]{1,0:T(8,128)(2,1)}, u32[]{:S(2)}) copy-start(bf16[8,512]{1,0:T(8,128)(2,1)} %copy-done.17) | copy-start | bytes 24580
  297.6 76.4 %copy-start.20 = (bf16[8,512]{1,0:T(8,128)(2,1)S(1)}, bf16[8,512]{1,0:T(8,128)(2,1)}, u32[]{:S(2)}) copy-start(bf16[8,512]{1,0:T(8,128)(2,1)} %copy-done.19) | copy-start | bytes 24580
  297.6 76.4 %copy-start.22 = (bf16[8,512]{1,0:T(8,128)(2,1)S(1)}, bf16[8,512]{1,0:T(8,128)(2,1)}, u32[]{:S(2)}) copy-start(bf16[8,512]{1,0:T(8,128)(2,1)} %copy-done.21) | copy-start | bytes 24580
  297.7 76.4 %copy-start.24 = (pred[8]{0:T(512)(128)(4,1)S(1)}, pred[8]{0:T(512)(128)(4,1)}, u32[]{:S(2)}) copy-start(pred[8]{0:T(512)(128)(4,1)} %get-tuple-element.132) | copy-start | bytes 28
  308.9 17.7 %copy-start.4 = (bf16[2,512,4,128]{1,3,2,0:T(8,128)(2,1)S(1)}, bf16[2,512,4,128]{1,3,2,0:T(8,128)(2,1)}, u32[]{:S(2)}) copy-start(bf16[2,512,4,128]{1,3,2,0:T(8,128)(2,1)} %get-tuple-element.207) | copy-start | bytes 3145732 | tf_op jit(solution)/shard_map/while
  346.6 17.7 %copy-start.4 = (bf16[2,512,4,128]{1,3,2,0:T(8,128)(2,1)S(1)}, bf16[2,512,4,128]{1,3,2,0:T(8,128)(2,1)}, u32[]{:S(2)}) copy-start(bf16[2,512,4,128]{1,3,2,0:T(8,128)(2,1)} %get-tuple-element.207) | copy-start | bytes 3145732 | tf_op jit(solution)/shard_map/while
  (7 other events, 4.3 us)
Sparse Core Ops, SparseCore 0:
  56.9 31.3 all-gather.1
Sparse Core Ops, SparseCore 1:
  374.0 18.3 reduce-scatter.3
where the time goes:
time: 404 us; the launch traced here: 401 us
  waiting for transfers between devices  218 us (54%)
  matrix products  62.5 us (15%)
  other arithmetic  57.6 us (14%)
  local copies, waits for them, and re-layouts  34.7 us (9%)
  between operations  16 us (4%)
  starting transfers between devices  10.9 us (3%)
    ppermute x5, waiting for transfers between devices, from_partner(): return lax.ppermute(value, axis, pairs)  212 us
    sub x2, other arithmetic, attend(): exp_scores = jnp.exp(scores - slot_top)  35.3 us
    unnamed x63, local copies, waits for them, and re-layouts  20.2 us
    dot_general x2, matrix products, attend(): jnp.einsum('thgd,phd->hgtp', query_full, keys_full, preferred_element_typ...  19.5 us
    dot_general x2, matrix products, attend(): jnp.einsum('hgtp,phd->thgd', prob_weights, values_full, preferred_element...  13.2 us
    dot_general x1, matrix products, body(): jnp.einsum('er,rcx->ecx', pick_rows, final_cache, preferred_element_type=...  11.7 us
    select_n x1, other arithmetic, body(): new_cache = jnp.where(finished_row[:, None, None], padded, final_cache)  9.06 us
  transfers between devices with their start and end apart: 8, of which 4 were waited for; matrix products, arithmetic and copies ran while one was open for 14% of the time, Pallas kernels for 0%

commit v1 on v0

v1 whole, which is shorter than its diff:
```python
import functools
import math

import jax
import jax.numpy as jnp
from jax import lax
from jax.experimental import pallas as pl
from jax.experimental.pallas import tpu as pltpu
from jax.sharding import PartitionSpec as P

GROUP = 8
D_HEAD = 128
HALF = 64
SCALE = 1.0 / math.sqrt(D_HEAD)
NT = (((1,), (1,)), ((), ()))


def from_partner(value, axis, apart):
    mask = 2**apart
    pairs = [(source, source ^ mask) for source in range(lax.axis_size(axis))]
    return lax.ppermute(value, axis, pairs)


def partial_kernel(heads, meta_ref, q_ref, kv_ref, out_ref):
    del meta_ref
    for h in range(heads):
        tile = kv_ref[0, :, h * D_HEAD : (h + 1) * D_HEAD]
        out_ref[0, h] = lax.dot_general(q_ref[0, h], tile, NT, preferred_element_type=jnp.float32)


def soft_kernel(heads, meta_ref, q_ref, kv_ref, other_ref, weight_ref, out_ref):
    row = meta_ref[0] + pl.program_id(0)
    length = meta_ref[1 + row]
    shape = other_ref.shape[2:]
    step = lax.broadcasted_iota(jnp.int32, shape, 0) // GROUP
    seen = lax.broadcasted_iota(jnp.int32, shape, 1) <= length + step
    for h in range(heads):
        tile = kv_ref[0, :, h * D_HEAD : (h + 1) * D_HEAD]
        mine = lax.dot_general(q_ref[0, h], tile, NT, preferred_element_type=jnp.float32)
        score = jnp.where(seen, (mine + other_ref[0, h]) * SCALE, -jnp.inf)
        score = jnp.exp(score - jnp.max(score, axis=-1, keepdims=True))
        weight = (score / jnp.sum(score, axis=-1, keepdims=True)).astype(jnp.bfloat16)
        weight_ref[0, h] = weight
        out_ref[0, h] = jnp.dot(weight, tile, preferred_element_type=jnp.float32)


def value_kernel(heads, meta_ref, weight_ref, kv_ref, out_ref):
    del meta_ref
    for h in range(heads):
        tile = kv_ref[0, :, h * D_HEAD : (h + 1) * D_HEAD]
        out_ref[0, h] = jnp.dot(weight_ref[0, h], tile, preferred_element_type=jnp.float32)


def row_call(kernel, meta, operands, kinds, out_kinds, rows, flops):
    def spec(shape, kind):
        tail = (0,) * (len(shape) - 1)
        if kind == "all":
            return pl.BlockSpec((1,) + shape[1:], lambda i, meta: (meta[0] + i,) + tail)
        return pl.BlockSpec((1,) + shape[1:], lambda i, meta: (i,) + tail)

    return pl.pallas_call(
        kernel,
        out_shape=out_kinds,
        grid_spec=pltpu.PrefetchScalarGridSpec(
            num_scalar_prefetch=1,
            grid=(rows,),
            in_specs=[spec(x.shape, k) for x, k in zip(operands, kinds)],
            out_specs=[spec(x.shape, "half") for x in out_kinds],
        ),
        cost_estimate=pl.CostEstimate(flops=flops, bytes_accessed=4 << 20, transcendentals=1 << 18),
    )(meta, *operands)


def verify_kernel(block, span_ref, qm_ref, qo_ref, key_ref, u_ref, out_ref):
    @pl.when(pl.program_id(0) == 0)
    def _():
        out_ref[...] = jnp.zeros_like(out_ref)

    span = span_ref[0]
    for tb in range(qm_ref.shape[0] // block):
        low, high = tb * block, (tb + 1) * block

        @pl.when(span > low)
        def _():
            query = jnp.concatenate([qm_ref[low:high], qo_ref[low:high]], axis=1)
            t = lax.broadcasted_iota(jnp.int32, (block, high), 0) + low
            p = lax.broadcasted_iota(jnp.int32, (block, high), 1)
            allowed = (p <= t) & (p < jnp.maximum(span, 1))
            total = jnp.zeros((block, 1), jnp.float32)
            for g in range(2):
                score = lax.dot_general(
                    query, key_ref[0, g, :high], NT, preferred_element_type=jnp.float32
                )
                score = jnp.where(allowed, score, -jnp.inf)
                top = jnp.max(score, axis=-1, keepdims=True)
                grown = jnp.exp2((score - top) * (SCALE * math.log2(math.e)))
                weighed = jnp.sum(grown * u_ref[0, g : g + 1, :high], axis=-1, keepdims=True)
                total += weighed / jnp.sum(grown, axis=-1, keepdims=True)
            out_ref[low:high] += jnp.broadcast_to(total, (block, 128))


def verify_call(span, q_mine, q_other, keys, u_pairs):
    context_len = q_mine.shape[0]
    pairs = u_pairs.shape[0]
    per_head = pairs // keys.shape[0]
    return pl.pallas_call(
        functools.partial(verify_kernel, 128),
        out_shape=jax.ShapeDtypeStruct((context_len, 128), jnp.float32),
        grid_spec=pltpu.PrefetchScalarGridSpec(
            num_scalar_prefetch=1,
            grid=(pairs,),
            in_specs=[
                pl.BlockSpec((context_len, 128), lambda i, s: (0, i)),
                pl.BlockSpec((context_len, 128), lambda i, s: (0, i)),
                pl.BlockSpec((1,) + keys.shape[1:], lambda i, s: (i // per_head, 0, 0, 0)),
                pl.BlockSpec((1, 2, context_len), lambda i, s: (i, 0, 0)),
            ],
            out_specs=pl.BlockSpec((context_len, 128), lambda i, s: (0, 0)),
        ),
        compiler_params=pltpu.CompilerParams(vmem_limit_bytes=24 << 20),
        cost_estimate=pl.CostEstimate(
            flops=pairs * 8 * context_len * context_len * D_HEAD,
            bytes_accessed=8 << 20,
            transcendentals=pairs * context_len * context_len,
        ),
    )(span, q_mine, q_other, keys, u_pairs)


def body(kv_cache, new_kv, queries, verify_q, prompt_kv, readout, finish, dest, prompt, lengths):
    row_count, context_len, columns = kv_cache.shape
    step_count = new_kv.shape[0]
    slot_count = verify_q.shape[0]
    plen = prompt_kv.shape[1]
    kv_local = columns // (2 * HALF)
    tp_size = lax.axis_size("tensor")
    peer_count = lax.axis_size("dp")
    my_index = lax.axis_index("dp")
    side = lax.axis_index("tensor") // (tp_size // 2)
    pair_bit = tp_size.bit_length() - 2
    swap = functools.partial(from_partner, axis="tensor", apart=pair_bit)
    first_row = my_index * row_count
    my_finish = lax.dynamic_slice_in_dim(finish, first_row, row_count)
    my_dest = lax.dynamic_slice_in_dim(dest, first_row, row_count)
    my_prompt = lax.dynamic_slice_in_dim(prompt, first_row, row_count)
    my_length = lax.dynamic_slice_in_dim(lengths, first_row, row_count)

    position = jnp.arange(context_len)
    grown = kv_cache
    for step in range(step_count):
        hit = position[None, :] == my_length[:, None] + step
        grown = jnp.where(hit[:, :, None], new_kv[step][:, None, :], grown)

    half = row_count // 2
    step_queries = step_count * GROUP
    q_rows = queries.reshape(step_count, row_count, kv_local, GROUP, HALF)
    q_rows = q_rows.transpose(1, 2, 0, 3, 4).reshape(row_count, kv_local, step_queries, HALF)
    q_rows = jnp.pad(q_rows, ((0, 0), (0, 0), (0, 0), (0, HALF)))
    keep_meta = jnp.concatenate([(side * half)[None], my_length]).astype(jnp.int32)
    give_meta = jnp.concatenate([((1 - side) * half)[None], my_length]).astype(jnp.int32)
    flops = 2 * half * kv_local * step_queries * context_len * D_HEAD
    score_kind = jax.ShapeDtypeStruct((half, kv_local, step_queries, context_len), jnp.float32)
    weight_kind = jax.ShapeDtypeStruct(score_kind.shape, jnp.bfloat16)
    mixed_kind = jax.ShapeDtypeStruct((half, kv_local, step_queries, D_HEAD), jnp.float32)
    (given,) = row_call(
        functools.partial(partial_kernel, kv_local),
        give_meta, (q_rows, grown), ("all", "all"), [score_kind], half, flops,
    )
    other_part = swap(given)

    per_side = slot_count // 2
    keep_query = lax.dynamic_slice_in_dim(verify_q, side * per_side, per_side)
    other_query = swap(lax.dynamic_slice_in_dim(verify_q, (1 - side) * per_side, per_side))

    finished_row = my_finish < step_count
    rank = jnp.cumsum(finished_row.astype(jnp.int32)) - 1
    weight = readout.reshape(kv_local, GROUP, HALF)
    target = jnp.where(finished_row, my_dest // slot_count, -1)
    key_out = jnp.zeros((), jnp.bfloat16)
    u_out = jnp.zeros((), jnp.float32)
    peers = jnp.arange(peer_count)[:, None, None]
    picks = []
    for turn in range(2):
        is_turn = finished_row & (rank == turn)
        row = jnp.argmax(is_turn)
        goes = jnp.max(jnp.where(is_turn, target, -1))
        picks.append((is_turn, jnp.maximum(my_prompt[row], 0)))
        picked = lax.dynamic_index_in_dim(grown, row, 0, keepdims=False)
        picked = picked.reshape(context_len, kv_local, 2, HALF)
        keys = picked[:, :, 0, :].reshape(context_len, kv_local * HALF)
        u_part = jnp.einsum(
            "phd,hgd->hgp", picked[:, :, 1, :], weight, preferred_element_type=jnp.float32
        ).reshape(kv_local * GROUP, context_len)
        key_out = jnp.where(peers == goes, keys[None], key_out)
        u_out = jnp.where(peers == goes, u_part[None], u_out)
    key_in = lax.all_to_all(key_out, "dp", split_axis=0, concat_axis=0, tiled=True)
    u_in = lax.all_to_all(u_out, "dp", split_axis=0, concat_axis=0, tiled=True)
    wanted = my_index * slot_count + jnp.arange(slot_count)
    slot_hits = dest.reshape(peer_count, row_count)[None] == wanted[:, None, None]
    full_span = (lengths + finish + 1).reshape(peer_count, row_count)
    span_len = jnp.sum(jnp.where(slot_hits, full_span[None], 0), axis=(1, 2))
    source = jnp.argmax(jnp.any(slot_hits, axis=2), axis=1)

    def of_slots(array, first):
        return jnp.stack([
            lax.dynamic_index_in_dim(array, source[first + i], 0, keepdims=False)
            for i in range(per_side)
        ])

    first_keep, first_give = side * per_side, (1 - side) * per_side
    other_keys, other_u = swap((of_slots(key_in, first_give), of_slots(u_in, first_give)))
    keep_keys = of_slots(key_in, first_keep)
    u_full = of_slots(u_in, first_keep) + other_u

    def by_head(keys):
        return keys.reshape(per_side, context_len, kv_local, HALF).transpose(0, 2, 1, 3)

    mine, other = by_head(keep_keys), by_head(other_keys)
    blank = jnp.zeros_like(mine)
    key_pairs = jnp.stack([
        jnp.concatenate([mine, blank, other, blank], axis=-1),
        jnp.concatenate([blank, mine, blank, other], axis=-1),
    ], axis=2)

    weights, mixed_keep = row_call(
        functools.partial(soft_kernel, kv_local),
        keep_meta, (q_rows, grown, other_part), ("all", "all", "half"),
        [weight_kind, mixed_kind], half, 2 * flops,
    )
    other_weights = swap(weights)

    slot_rewards = []
    for i in range(per_side):
        slot_span = span_len[first_keep + i]
        reward = verify_call(
            slot_span[None].astype(jnp.int32), keep_query[i], other_query[i], key_pairs[i],
            u_full[i].reshape(kv_local * GROUP // 2, 2, context_len),
        )[:, 0]
        slot_rewards.append(jnp.where(position < slot_span, reward, 0.0))
    kept = jnp.stack(slot_rewards)
    nothing = jnp.zeros_like(kept)
    partial_value = jnp.concatenate(
        [jnp.where(side == 0, kept, nothing), jnp.where(side == 0, nothing, kept)]
    )
    rewards = lax.psum_scatter(partial_value, "tensor", scatter_dimension=1, tiled=True)

    (mixed_give,) = row_call(
        functools.partial(value_kernel, kv_local),
        give_meta, (other_weights, grown), ("half", "all"), [mixed_kind], half, flops,
    )
    mixed_keep, mixed_give = mixed_keep[..., HALF:], mixed_give[..., HALF:]
    mixed = jnp.concatenate([
        jnp.where(side == 0, mixed_keep, mixed_give), jnp.where(side == 0, mixed_give, mixed_keep)
    ]).reshape(row_count, kv_local, step_count, GROUP, HALF).transpose(2, 0, 1, 3, 4)
    live = jnp.arange(step_count)[:, None] <= my_finish[None, :]
    decoded = jnp.where(live[:, :, None, None, None], mixed, 0.0)
    decoded = decoded.astype(jnp.bfloat16).reshape(queries.shape)

    prompts = lax.all_gather(prompt_kv, "dp", axis=0, tiled=True)
    new_cache = grown
    for is_turn, which in picks:
        refill = lax.dynamic_index_in_dim(prompts, which, 0, keepdims=False)
        refill = jnp.pad(refill, ((0, context_len - plen), (0, 0)))
        new_cache = jnp.where(is_turn[:, None, None], refill[None], new_cache)
    return (decoded, new_cache, rewards)


def solution(mesh):
    placed = (
        P("dp", None, "tensor"),
        P(None, "dp", "tensor"),
        P(None, "dp", "tensor"),
        P("dp", None, "tensor"),
        P("dp", None, "tensor"),
        P("tensor"),
        P(),
        P(),
        P(),
        P(),
    )
    return jax.shard_map(
        body,
        mesh=mesh,
        in_specs=placed,
        out_specs=(P(None, "dp", "tensor"), P("dp", None, "tensor"), P("dp", "tensor")),
        check_vma=False,
    )
```

time: 404 us -> 318 us (0.79); the launches traced: 401 us -> 319 us
  matrix products: 62.5 us -> 0.29 us
  Pallas kernels: 0 us -> 40.1 us
  other arithmetic: 57.6 us -> 21.8 us
  waiting for transfers between devices: 218 us -> 193 us
  local copies, waits for them, and re-layouts: 34.7 us -> 23.2 us
  between operations: 16 us -> 23.1 us
  starting transfers between devices: 10.9 us -> 17.6 us
    ppermute x5, waiting for transfers between devices: 212 us -> 143 us  [from_partner(): return lax.ppermute(value, axis, pairs)]
    dot_general x13 -> x2, matrix products: 62.5 us -> 0.29 us  [body(): jnp.einsum('phd,hgd->hgp', picked[:, :, 1, :], weight, preferred_element_...]
    pallas_call x0 -> x4, Pallas kernels: none -> 40.1 us  [the longest x1 22.5 us: verify_call(): pl.pallas_call(functools.partial(verify_kernel, 128), out_shape=jax.Shape...]
    sub x2 -> x0, other arithmetic: 35.3 us -> none  [attend(): exp_scores = jnp.exp(scores - slot_top)]
    unnamed x3, waiting for transfers between devices: 5.89 us -> 27.1 us
    all_gather x1, waiting for transfers between devices: 0.02 us -> 17.8 us  [body(): prompts = lax.all_gather(prompt_kv, 'dp', axis=0, tiled=True)]
    unnamed x63 -> x24, local copies, waits for them, and re-layouts: 20.2 us -> 7.63 us
    dynamic_slice x3 -> x9, local copies, waits for them, and re-layouts: 1.36 us -> 8.97 us  [the longest x1 4 us: body(): lax.dynamic_slice_in_dim(verify_q, (1 - side) * per_side, per_side)]
  transfers between devices with their start and end apart: 8 -> 9, of which waited for: 4 -> 5; matrix products, arithmetic and copies ran while one was open for 14% -> 8% of each run, Pallas kernels for 0% -> 6%
where the time goes in v1:
time: 318 us; the launch traced here: 319 us
  waiting for transfers between devices  193 us (61%)
  Pallas kernels  40.1 us (13%)
  local copies, waits for them, and re-layouts  23.2 us (7%)
  between operations  23.1 us (7%)
  other arithmetic  21.8 us (7%)
  starting transfers between devices  17.6 us (6%)
    ppermute x5, waiting for transfers between devices, from_partner(): return lax.ppermute(value, axis, pairs)  143 us
    unnamed x3, waiting for transfers between devices  27.1 us
    pallas_call x1, Pallas kernels, verify_call(): pl.pallas_call(functools.partial(verify_kernel, 128), out_shape=jax.Shape...  22.5 us
    all_gather x1, waiting for transfers between devices, body(): prompts = lax.all_gather(prompt_kv, 'dp', axis=0, tiled=True)  17.8 us
    pallas_call x3, Pallas kernels, row_call(): pl.pallas_call(kernel, out_shape=out_kinds, grid_spec=pltpu.PrefetchScala...  17.6 us
    select_n x1, other arithmetic, body(): new_cache = jnp.where(is_turn[:, None, None], refill[None], new_cache)  7.75 us
    unnamed x24, local copies, waits for them, and re-layouts  7.63 us
    all_to_all x1, starting transfers between devices, body(): lax.all_to_all(key_out, 'dp', split_axis=0, concat_axis=0, tiled=True)  6.65 us
  transfers between devices with their start and end apart: 9, of which 5 were waited for; matrix products, arithmetic and copies ran while one was open for 8% of the time, Pallas kernels for 6%

profile of v1, /device:TPU:6, one launch (start us, length us, event | category | flops | bytes accessed | tf_op | source)
XLA Modules:
  0.0 319.5 jit_solution(2927571297109459912)
XLA Ops:
  14.5 1.4 fusion.5
  20.3 17.8 %all-gather.2.cloned.1.call-done = bf16[8,256,512]{2,1,0:T(8,128)(2,1)} async-done(((bf16[1,256,512]{2,1,0:T(8,128)(2,1)}), bf16[8,256,512]{2,1,0:T(8,128)(2,1)}) %all-gather.2.cloned.1.call-update) | async-done | bytes 2097168 | tf_op jit(solution)/shard_map/all_gather | solution.py:258
  38.1 1.1 dynamic-slice_bitcast_fusion.2
  39.3 7.7 %select_select_fusion = (bf16[8,512,512]{2,1,0:T(8,128)(2,1)}, bf16[8,512,512]{2,1,0:T(8,128)(2,1)S(1)}) fusion(pred[8]{0:T(512)(128)(4,1)S(1)} %get-tuple-element.16, pred[8]{0:T(512)(128)(4,1)S(1)} %get-tuple-element.15, bf16[512,512]{1,0:T(8,128)(2,1)S(1)} %pad.13, bf16[512,512]{1,0:T(8,128)(2,1)S(1)} %pad.12, bf16[8,512,512]{2,1,0:T(8,128)(2,1)} %param.10, ...), kind=kLoop, calls=%fused_computation | loop fusion | flops 12582912 | bytes 13680656 | tf_op jit(solution)/shard_map/jit(_where)/select_n | solution.py:263
  47.0 1.9 copy-done
  49.7 0.9 select_select_fusion.3
  50.7 4.9 %all-to-all-start.1 = ((f32[8,32,512]{2,1,0:T(8,128)}), f32[8,32,512]{2,1,0:T(8,128)S(1)}, u32[]{:S(2)}, u32[]{:S(2)}) async-start(f32[8,32,512]{2,1,0:T(8,128)} %select_select_fusion.3), calls=%async_computation.1 | async-start | bytes 1048576 | tf_op jit(solution)/shard_map/all_to_all | solution.py:196
  55.6 1.7 select_select_fusion.2
  57.3 5.6 %all-to-all-done.1 = f32[8,32,512]{2,1,0:T(8,128)S(1)} async-done(((f32[8,32,512]{2,1,0:T(8,128)}), f32[8,32,512]{2,1,0:T(8,128)S(1)}, u32[]{:S(2)}, u32[]{:S(2)}) %all-to-all-start.1) | async-done | bytes 524320 | tf_op jit(solution)/shard_map/all_to_all | solution.py:196
  62.9 0.8 copy-done.2
  63.7 6.6 %all-to-all-start = ((bf16[8,512,256]{1,2,0:T(8,128)(2,1)}), bf16[8,512,256]{1,2,0:T(8,128)(2,1)}, u32[]{:S(2)}, u32[]{:S(2)}) async-start(bf16[8,512,256]{1,2,0:T(8,128)(2,1)} %select_select_fusion.2), calls=%async_computation | async-start | bytes 4194304 | tf_op jit(solution)/shard_map/all_to_all | solution.py:195
  72.1 4.8 %shard_map.121 = f32[4,4,32,512]{3,2,1,0:T(8,128)} custom-call(s32[9]{0:T(128)} %get-tuple-element.48.meta_ref, bf16[8,4,32,128]{3,2,1,0:T(8,128)(2,1)} %pad.11.q_ref, bf16[8,512,512]{2,1,0:T(8,128)(2,1)} %copy-done), custom_call_target="tpu_custom_call" | custom-call | flops 67108864 | bytes 4194304 | tf_op jit(solution)/shard_map/pallas_call | solution.py:61
  76.9 2.5 collective-permute-start
  79.4 4.0 %constant_dynamic-slice_fusion.5 = (bf16[1,512,2048]{2,1,0:T(8,128)(2,1)}, bf16[512,2048]{1,0:T(8,128)(2,1)S(1)}) fusion(bf16[2,512,2048]{2,1,0:T(8,128)(2,1)} %param.13, s32[]{:T(128)S(6)} %select_n.194, s32[]{:T(128)S(6)} %select_n.193), kind=kLoop, calls=%fused_computation.43 | loop fusion | bytes 8388616 | tf_op jit(solution)/shard_map/dynamic_slice | solution.py:172
  88.2 83.3 %collective-permute-done.other_ref = f32[4,4,32,512]{3,2,1,0:T(8,128)S(1)} collective-permute-done((f32[4,4,32,512]{3,2,1,0:T(8,128)}, f32[4,4,32,512]{3,2,1,0:T(8,128)S(1)}, u32[]{:S(2)}, u32[]{:S(2)}) %collective-permute-start) | collective-permute-done | bytes 1048608 | tf_op jit(solution)/shard_map/ppermute | solution.py:21
  171.5 1.0 copy-done.1
  172.6 8.2 %shard_map.122 = (bf16[4,4,32,512]{3,2,1,0:T(8,128)(2,1)}, f32[4,4,32,128]{3,2,1,0:T(8,128)}) custom-call(s32[9]{0:T(128)} %get-tuple-element.47.meta_ref, bf16[8,4,32,128]{3,2,1,0:T(8,128)(2,1)} %pad.11.q_ref, bf16[8,512,512]{2,1,0:T(8,128)(2,1)} %copy-done, f32[4,4,32,512]{3,2,1,0:T(8,128)} %copy-done.1), custom_call_target="tpu_custom_call" | custom-call | flops 134217728 | bytes 4194304 | tf_op jit(solution)/shard_map/pallas_call | solution.py:61
  182.9 0.8 constant_dynamic-slice_fusion
  183.7 2.9 collective-permute-start.4
  186.7 1.1 constant_dynamic-slice_fusion.2
  187.8 59.6 %collective-permute-done.4 = f32[1,32,512]{2,1,0:T(8,128)S(1)} collective-permute-done((f32[1,32,512]{2,1,0:T(8,128)S(1)}, f32[1,32,512]{2,1,0:T(8,128)S(1)}, u32[]{:S(2)}, u32[]{:S(2)}) %collective-permute-start.4) | collective-permute-done | bytes 65568 | tf_op jit(solution)/shard_map/ppermute | solution.py:21
  247.4 0.8 dynamic-slice_add_fusion
  248.3 0.8 copy-done.3
  249.1 4.6 %shard_map.123 = f32[4,4,32,128]{3,2,1,0:T(8,128)} custom-call(s32[9]{0:T(128)} %get-tuple-element.48.meta_ref, bf16[4,4,32,512]{3,2,1,0:T(8,128)(2,1)} %copy-done.3, bf16[8,512,512]{2,1,0:T(8,128)(2,1)} %copy-done), custom_call_target="tpu_custom_call" | custom-call | flops 67108864 | bytes 4194304 | tf_op jit(solution)/shard_map/pallas_call | solution.py:61
  253.7 1.9 slice_select_fusion.1
  256.5 1.2 copy.41
  257.8 1.4 maximum_bitcast_fusion.1
  259.5 22.5 %shard_map.124 = f32[512,128]{1,0:T(8,128)S(1)} custom-call(s32[1]{0:T(128)} %dynamic_slice.73.span_ref, bf16[512,2048]{1,0:T(8,128)(2,1)S(1)} %get-tuple-element.26.qm_ref, bf16[512,2048]{1,0:T(8,128)(2,1)} %bitcast.19.qo_ref, bf16[4,2,512,256]{3,2,1,0:T(8,128)(2,1)S(1)} %maximum_bitcast_fusion.key_ref, f32[16,2,512]{2,1,0:T(2,128)S(1)} %reshape_squeeze.3.u_ref), custom_call_target="tpu_custom_call" | custom-call | flops 4294967296 | bytes 8388608 | tf_op jit(solution)/shard_map/pallas_call | solution.py:106
  282.8 0.8 copy.45
  283.8 0.9 reshape.234
  284.8 26.4 %reduce-scatter.4.cloned.1.call-done = f32[128,2]{1,0:T(8,128)} async-done(((f32[512,2]{1,0:T(8,128)}), f32[128,2]{1,0:T(8,128)}) %reduce-scatter.4.cloned.1.call-update) | async-done | bytes 1040
  311.2 1.5 copy.46
  (76 shorter events, 14.8 us)
Async XLA Ops:
  7.2 31.0 %all-gather.2.cloned.1.call-start = ((), (), s32[]{:S(2)}) async-start(), calls=%async_computation.3 | async-start | bytes 2359296 | tf_op jit(solution)/shard_map/all_gather | solution.py:258
  47.0 1.9 copy-start
  50.7 12.3 %all-to-all-start.1 = ((f32[8,32,512]{2,1,0:T(8,128)}), f32[8,32,512]{2,1,0:T(8,128)S(1)}, u32[]{:S(2)}, u32[]{:S(2)}) async-start(f32[8,32,512]{2,1,0:T(8,128)} %select_select_fusion.3), calls=%async_computation.1 | async-start | bytes 1048576 | tf_op jit(solution)/shard_map/all_to_all | solution.py:196
  57.3 13.1 %copy-start.7 = (bf16[4,8,2048]{2,1,0:T(8,128)(2,1)S(1)}, bf16[4,8,2048]{2,1,0:T(8,128)(2,1)}, u32[]{:S(2)}) copy-start(bf16[4,8,2048]{2,1,0:T(8,128)(2,1)} %param.12) | copy-start | bytes 393220
  62.9 0.8 copy-start.2
  63.7 122.9 %all-to-all-start = ((bf16[8,512,256]{1,2,0:T(8,128)(2,1)}), bf16[8,512,256]{1,2,0:T(8,128)(2,1)}, u32[]{:S(2)}, u32[]{:S(2)}) async-start(bf16[8,512,256]{1,2,0:T(8,128)(2,1)} %select_select_fusion.2), calls=%async_computation | async-start | bytes 4194304 | tf_op jit(solution)/shard_map/all_to_all | solution.py:195
  70.4 240.8 %reduce-scatter.4.cloned.1.call-start = ((), (), s32[]{:S(2)}) async-start(), calls=%async_computation.4 | async-start | bytes 327680
  76.9 7.0 %copy-start.8 = (s32[64]{0:T(128)S(1)}, s32[64]{0:T(128)}, u32[]{:S(2)}) copy-start(s32[64]{0:T(128)} %param.17) | copy-start | bytes 772
  76.9 11.1 %copy-start.9 = (s32[64]{0:T(128)S(1)}, s32[64]{0:T(128)}, u32[]{:S(2)}) copy-start(s32[64]{0:T(128)} %param.16) | copy-start | bytes 772
  76.9 11.1 %copy-start.10 = (s32[64]{0:T(128)S(1)}, s32[64]{0:T(128)}, u32[]{:S(2)}) copy-start(s32[64]{0:T(128)} %param.19) | copy-start | bytes 772
  76.9 94.6 %collective-permute-start = (f32[4,4,32,512]{3,2,1,0:T(8,128)}, f32[4,4,32,512]{3,2,1,0:T(8,128)S(1)}, u32[]{:S(2)}, u32[]{:S(2)}) collective-permute-start(f32[4,4,32,512]{3,2,1,0:T(8,128)} %shard_map.121), channel_id=1, source_target_pairs={{0,2},{1,3},{2,0},{3,1},{4,6},{5,7},{6,4},{7,5},{8,10},{9,11},{10,... | collective-permute-start | bytes 3145736 | tf_op jit(solution)/shard_map/ppermute | solution.py:21
  83.4 176.0 %collective-permute-start.2 = (bf16[1,512,2048]{2,1,0:T(8,128)(2,1)}, bf16[1,512,2048]{2,1,0:T(8,128)(2,1)}, u32[]{:S(2)}, u32[]{:S(2)}) collective-permute-start(bf16[1,512,2048]{2,1,0:T(8,128)(2,1)} %get-tuple-element.25), channel_id=1, source_target_pairs={{0,2},{1,3},{2,0},{3,1},{4,6},{5,7},{6,4},{7,5},{8,10},{9,11},{10,... | collective-permute-start | bytes 6291464 | tf_op jit(solution)/shard_map/ppermute | solution.py:21
  171.5 1.1 copy-start.1
  180.8 67.5 %collective-permute-start.1 = (bf16[4,4,32,512]{3,2,1,0:T(8,128)(2,1)}, bf16[4,4,32,512]{3,2,1,0:T(8,128)(2,1)S(1)}, u32[]{:S(2)}, u32[]{:S(2)}) collective-permute-start(bf16[4,4,32,512]{3,2,1,0:T(8,128)(2,1)} %get-tuple-element.9), channel_id=1, source_target_pairs={{0,2},{1,3},{2,0},{3,1},{4,6},{5,7},{6,4},{7,5},{8,10},{9,11},{10,... | collective-permute-start | bytes 1572872 | tf_op jit(solution)/shard_map/ppermute | solution.py:21
  183.7 63.6 %collective-permute-start.4 = (f32[1,32,512]{2,1,0:T(8,128)S(1)}, f32[1,32,512]{2,1,0:T(8,128)S(1)}, u32[]{:S(2)}, u32[]{:S(2)}) collective-permute-start(f32[1,32,512]{2,1,0:T(8,128)S(1)} %constant_dynamic-slice_fusion), channel_id=1, source_target_pairs={{0,2},{1,3},{2,0},{3,1},{4,6},{5,7},{6,4},{7,5},{8,10},{9,11},{10,... | collective-permute-start | bytes 196616 | tf_op jit(solution)/shard_map/ppermute | solution.py:21
  187.7 68.1 %collective-permute-start.3 = (bf16[1,512,256]{1,2,0:T(8,128)(2,1)S(1)}, bf16[1,512,256]{1,2,0:T(8,128)(2,1)S(1)}, u32[]{:S(2)}, u32[]{:S(2)}) collective-permute-start(bf16[1,512,256]{1,2,0:T(8,128)(2,1)S(1)} %get-tuple-element.28), channel_id=1, source_target_pairs={{0,2},{1,3},{2,0},{3,1},{4,6},{5,7},{6,4},{7,5},{8,10},{9,11},{10,... | collective-permute-start | bytes 786440 | tf_op jit(solution)/shard_map/ppermute | solution.py:21
  248.3 0.8 copy-start.3
  255.8 0.7 copy-start.6
  259.4 24.2 %copy-start.4 = (bf16[4,4,32,64]{3,2,1,0:T(8,128)(2,1)S(1)}, bf16[4,4,32,64]{3,2,1,0:T(8,128)(2,1)}, u32[]{:S(2)}) copy-start(bf16[4,4,32,64]{3,2,1,0:T(8,128)(2,1)} %get-tuple-element.33) | copy-start | bytes 196612
  259.5 24.2 %copy-start.5 = (bf16[4,4,32,64]{3,2,1,0:T(8,128)(2,1)S(1)}, bf16[4,4,32,64]{3,2,1,0:T(8,128)(2,1)}, u32[]{:S(2)}) copy-start(bf16[4,4,32,64]{3,2,1,0:T(8,128)(2,1)} %get-tuple-element.34) | copy-start | bytes 196612
Sparse Core Ops, SparseCore 0:
  9.9 28.1 all-gather.1
  283.8 27.3 reduce-scatter.3
